TPU v7x, 32 devices: a whole 2x2x4 slice. The times are simulated.
32 devices in a mesh: row: 8 (over y, x, core), col: 4 (over z).
Axes of the slice: x: 2, y: 2, z: 4, core: 2. Of those that a mesh axis runs over, the one named last changes fastest.
Arguments:
- traces: bfloat16 [4096, 782], P(('row', 'col')), may hold values from -60 to 60
- taps: float32 [16], replicated, may hold values from -1.5 to 1.5
Outputs:
- correlations: float32 [32, 4096, 4096], P(None, 'row', 'col')
All inputs are finite; a program needn't handle non-finite values.
Results may differ from a plain program's by a relative error of at most 0.0036.
Values may be sent and summed in bfloat16 or wider, within the bound.
A program may use at most 256 MiB of HBM per device.

v0:
```python
import math

import jax
import jax.numpy as jnp
from jax import lax
from jax.sharding import PartitionSpec as P

LAGS = 32


def from_root(array, axis, root):
    mine = lax.axis_index(axis) == root
    return lax.psum(jnp.where(mine, array, jnp.zeros_like(array)), axis)


def whiten(traces, taps, count):
    samples = traces.astype(jnp.float32)
    decimated = jnp.zeros((samples.shape[0], count), jnp.float32)
    for k in range(taps.shape[0]):
        decimated = decimated + taps[k] * samples[:, k : k + 2 * count - 1 : 2]
    centred = decimated - jnp.mean(decimated, axis=1, keepdims=True)
    spread = jnp.sqrt(jnp.mean(centred * centred, axis=1, keepdims=True) + 1e-06)
    return (centred / spread).astype(jnp.bfloat16)


def on_device(traces, taps):
    count = (traces.shape[1] - taps.shape[0] + 2) // 2
    factor = lax.axis_size("row") // lax.axis_size("col")
    column = lax.axis_index("col")
    source = lax.all_gather(traces, "col", axis=0, tiled=True)
    first_block = whiten(source, taps, count)
    pieces = [from_root(source, "row", factor * column + k) for k in range(factor)]
    second_block = jnp.concatenate(pieces, axis=0)
    second_block = whiten(second_block, taps, count)
    lag_count = LAGS
    width = count - lag_count + 1
    scale_factor = 1.0 / math.sqrt(width)
    left = first_block[:, :width]
    groups = []
    for group in range(lag_count // 8):
        shifted = jnp.stack(
            [second_block[:, group * 8 + lag : group * 8 + lag + width] for lag in range(8)], axis=0
        )
        product = jnp.einsum("in,ljn->lij", left, shifted, preferred_element_type=jnp.float32)
        groups.append(product * scale_factor)
    return jnp.concatenate(groups, axis=0)


def solution(mesh):
    placed = (P(("row", "col"), None), P())
    return jax.shard_map(
        on_device, mesh=mesh, in_specs=placed, out_specs=P(None, "row", "col"), check_vma=False
    )
```

profile of v0, /device:TPU:0, one launch (start us, length us, event | category | flops | bytes accessed | tf_op | source)
XLA Modules:
  0.0 332.4 jit_solution(4783237983157764529)
XLA Ops:
  6.5 0.0 all-reduce.3.cloned.1.call-start
  6.5 20.8 %all_gather.3 = bf16[512,782]{0,1:T(8,128)(2,1)S(1)} all-gather(bf16[128,782]{0,1:T(8,128)(2,1)} %param.2), channel_id=1, replica_groups=mesh['row'=8,'col'=4] {'col'}, dimensions={0}, use_global_device_ids=true | all-gather | bytes 1000960 | tf_op jit(solution)/shard_map/all_gather | solution.py:30
  27.3 1.3 broadcast_select_fusion.1
  28.6 0.0 all-reduce.3.cloned.1.call-update
  28.6 0.9 slice.301
  29.5 0.9 slice.302
  30.4 0.9 slice.303
  31.3 2.9 slice.304
  34.2 2.8 slice.305
  37.1 2.8 slice.306
  39.9 2.8 slice.307
  42.7 2.8 slice.308
  45.5 2.8 slice.309
  48.4 2.9 slice.310
  51.2 2.9 slice.311
  54.1 2.9 slice.312
  57.0 2.9 slice.313
  59.8 2.8 slice.314
  62.6 2.8 slice.299
  65.4 2.8 slice.300
  68.2 0.0 copy-done.4
  68.2 0.7 fusion.39
  68.9 15.6 %fusion.37 = (f32[512]{0:T(512)S(1)}, f32[512,384]{0,1:T(8,128)S(1)}) fusion(f32[512,384]{0,1:T(8,128)} %slice.314, f32[]{:T(128)} %bitcast.15, f32[512,384]{0,1:T(8,128)} %slice.313, f32[]{:T(128)} %bitcast.14, f32[512,384]{0,1:T(8,128)} %slice.312, f32[]{:T(128)} %bitcast.13, f32[512,384]{0,1:T(8,128)} %slice.311, f32[]{:T(128)} %bitcast.12, ...), kind=kLoop, calls=%fused_computation.88 | loop fusion | flops 6290944 | bytes 13371456 | tf_op jit(solution)/shard_map/reduce_sum | solution.py:21
  84.5 0.1 multiply_reduce_fusion.1
  84.6 0.9 fusion.24
  85.5 1.4 all-reduce.3.cloned.1.call-done
  86.9 1.8 maximum_convert_fusion
  88.7 4.3 %slice.290 = f32[1024,384]{0,1:T(8,128)} slice(f32[1024,782]{0,1:T(8,128)S(1)} %maximum_convert_fusion), slice={[0:1024:1], [15:782:2]} | slice | bytes 3145728 | tf_op jit(solution)/shard_map/slice | solution.py:20
  93.0 4.3 %slice.288 = f32[1024,384]{0,1:T(8,128)} slice(f32[1024,782]{0,1:T(8,128)S(1)} %maximum_convert_fusion), slice={[0:1024:1], [14:781:2]} | slice | bytes 3145728 | tf_op jit(solution)/shard_map/slice | solution.py:20
  97.3 4.3 %slice.286 = f32[1024,384]{0,1:T(8,128)} slice(f32[1024,782]{0,1:T(8,128)S(1)} %maximum_convert_fusion), slice={[0:1024:1], [13:780:2]} | slice | bytes 3145728 | tf_op jit(solution)/shard_map/slice | solution.py:20
  101.6 4.3 %slice.284 = f32[1024,384]{0,1:T(8,128)} slice(f32[1024,782]{0,1:T(8,128)S(1)} %maximum_convert_fusion), slice={[0:1024:1], [12:779:2]} | slice | bytes 3145728 | tf_op jit(solution)/shard_map/slice | solution.py:20
  105.9 4.4 %slice.282 = f32[1024,384]{0,1:T(8,128)} slice(f32[1024,782]{0,1:T(8,128)S(1)} %maximum_convert_fusion), slice={[0:1024:1], [11:778:2]} | slice | bytes 3145728 | tf_op jit(solution)/shard_map/slice | solution.py:20
  110.2 4.3 %slice.280 = f32[1024,384]{0,1:T(8,128)} slice(f32[1024,782]{0,1:T(8,128)S(1)} %maximum_convert_fusion), slice={[0:1024:1], [10:777:2]} | slice | bytes 3145728 | tf_op jit(solution)/shard_map/slice | solution.py:20
  114.5 4.3 %slice.278 = f32[1024,384]{0,1:T(8,128)} slice(f32[1024,782]{0,1:T(8,128)S(1)} %maximum_convert_fusion), slice={[0:1024:1], [9:776:2]} | slice | bytes 3145728 | tf_op jit(solution)/shard_map/slice | solution.py:20
  118.8 4.2 %slice.276 = f32[1024,384]{0,1:T(8,128)} slice(f32[1024,782]{0,1:T(8,128)S(1)} %maximum_convert_fusion), slice={[0:1024:1], [8:775:2]} | slice | bytes 3145728 | tf_op jit(solution)/shard_map/slice | solution.py:20
  123.0 4.3 %slice.274 = f32[1024,384]{0,1:T(8,128)} slice(f32[1024,782]{0,1:T(8,128)S(1)} %maximum_convert_fusion), slice={[0:1024:1], [7:774:2]} | slice | bytes 3145728 | tf_op jit(solution)/shard_map/slice | solution.py:20
  127.3 4.3 %slice.272 = f32[1024,384]{0,1:T(8,128)} slice(f32[1024,782]{0,1:T(8,128)S(1)} %maximum_convert_fusion), slice={[0:1024:1], [6:773:2]} | slice | bytes 3145728 | tf_op jit(solution)/shard_map/slice | solution.py:20
  131.6 4.3 %slice.270 = f32[1024,384]{0,1:T(8,128)} slice(f32[1024,782]{0,1:T(8,128)S(1)} %maximum_convert_fusion), slice={[0:1024:1], [5:772:2]} | slice | bytes 3145728 | tf_op jit(solution)/shard_map/slice | solution.py:20
  135.9 4.3 %slice.268 = f32[1024,384]{0,1:T(8,128)} slice(f32[1024,782]{0,1:T(8,128)S(1)} %maximum_convert_fusion), slice={[0:1024:1], [4:771:2]} | slice | bytes 3145728 | tf_op jit(solution)/shard_map/slice | solution.py:20
  140.2 4.3 %slice.266 = f32[1024,384]{0,1:T(8,128)} slice(f32[1024,782]{0,1:T(8,128)S(1)} %maximum_convert_fusion), slice={[0:1024:1], [3:770:2]} | slice | bytes 3145728 | tf_op jit(solution)/shard_map/slice | solution.py:20
  144.6 4.3 %slice.264 = f32[1024,384]{0,1:T(8,128)} slice(f32[1024,782]{0,1:T(8,128)S(1)} %maximum_convert_fusion), slice={[0:1024:1], [2:769:2]} | slice | bytes 3145728 | tf_op jit(solution)/shard_map/slice | solution.py:20
  148.9 4.2 %slice.262 = f32[1024,384]{0,1:T(8,128)} slice(f32[1024,782]{0,1:T(8,128)S(1)} %maximum_convert_fusion), slice={[0:1024:1], [1:768:2]} | slice | bytes 3145728 | tf_op jit(solution)/shard_map/slice | solution.py:20
  153.1 4.2 %slice.260 = f32[1024,384]{0,1:T(8,128)} slice(f32[1024,782]{0,1:T(8,128)S(1)} %maximum_convert_fusion), slice={[0:1024:1], [0:767:2]} | slice | bytes 3145728 | tf_op jit(solution)/shard_map/slice | solution.py:20
  157.3 21.6 %fusion.38 = (f32[1024]{0:T(1024)S(1)}, f32[1024,384]{0,1:T(8,128)S(1)}) fusion(f32[1024,384]{0,1:T(8,128)} %slice.290, f32[]{:T(128)} %bitcast.15, f32[1024,384]{0,1:T(8,128)} %slice.288, f32[]{:T(128)} %bitcast.14, f32[1024,384]{0,1:T(8,128)} %slice.286, f32[]{:T(128)} %bitcast.13, f32[1024,384]{0,1:T(8,128)} %slice.284, f32[]{:T(128)} %bitcast.12, ...), kind=kLoop, calls=%fused_computation.89 | loop fusion | flops 12581888 | bytes 26742848 | tf_op jit(solution)/shard_map/reduce_sum | solution.py:21
  178.9 0.2 multiply_reduce_fusion
  179.2 0.2 divide_convert_fusion
  179.4 0.3 fusion.32
  179.7 0.4 fusion.31
  180.1 0.4 fusion.30
  180.5 0.4 fusion.29
  180.9 0.4 fusion.28
  181.3 0.4 fusion.27
  181.7 0.4 fusion.26
  182.1 0.4 fusion.25
  182.5 0.0 copy-start
  182.6 2.6 copy-done
  185.1 2.5 copy-done.2
  187.7 5.1 %multiply_bitcast_fusion.3 = f32[8,512,1024]{1,2,0:T(8,128)S(1)} fusion(bf16[8,1024,353]{1,2,0:T(8,128)(2,1)S(1)} %get-tuple-element.15, bf16[512,353]{0,1:T(8,128)(2,1)S(1)} %copy-done.3), kind=kOutput, calls=%fused_computation.4 | convolution fusion | flops 2965372928 | bytes 22922240 | tf_op jit(solution)/shard_map/in,ljn->lij/dot_general | solution.py:44
  192.8 0.0 slice-start
  192.8 9.0 %multiply_bitcast_fusion = f32[8,512,1024]{1,2,0:T(8,128)} fusion(bf16[8,1024,353]{1,2,0:T(8,128)(2,1)S(1)} %get-tuple-element.16, bf16[512,353]{0,1:T(8,128)(2,1)S(1)} %copy-done.3), kind=kOutput, calls=%fused_computation.1 | convolution fusion | flops 2965372928 | bytes 22922240 | tf_op jit(solution)/shard_map/in,ljn->lij/dot_general | solution.py:44
  201.9 8.5 %multiply_bitcast_fusion.1 = f32[8,512,1024]{1,2,0:T(8,128)} fusion(bf16[8,1024,353]{1,2,0:T(8,128)(2,1)S(1)} %copy-done.1, bf16[512,353]{0,1:T(8,128)(2,1)S(1)} %copy-done.3), kind=kOutput, calls=%fused_computation.2 | convolution fusion | flops 2965372928 | bytes 22922240 | tf_op jit(solution)/shard_map/in,ljn->lij/dot_general | solution.py:44
  210.4 8.5 %multiply_bitcast_fusion.2 = f32[8,512,1024]{1,2,0:T(8,128)} fusion(bf16[8,1024,353]{1,2,0:T(8,128)(2,1)S(1)} %bitcast.166, bf16[512,353]{0,1:T(8,128)(2,1)S(1)} %copy-done.3), kind=kOutput, calls=%fused_computation.3 | convolution fusion | flops 2965372928 | bytes 22922240 | tf_op jit(solution)/shard_map/in,ljn->lij/dot_general | solution.py:44
  218.8 40.9 %pad_maximum_fusion = f32[32,512,1024]{1,2,0:T(8,128)} fusion(f32[8,512,1024]{1,2,0:T(8,128)} %multiply_bitcast_fusion, f32[8,512,1024]{1,2,0:T(8,128)} %multiply_bitcast_fusion.1, f32[8,512,1024]{1,2,0:T(8,128)} %multiply_bitcast_fusion.2, f32[8,512,1024]{1,2,0:T(8,128)S(1)} %multiply_bitcast_fusion.3), kind=kLoop, calls=%fused_computation | loop fusion | flops 50331648 | bytes 134217728 | tf_op jit(solution)/shard_map/concatenate | solution.py:46
  259.7 65.8 %copy.3 = f32[32,512,1024]{2,1,0:T(8,128)} copy(f32[32,512,1024]{1,2,0:T(8,128)} %pad_maximum_fusion) | data formatting | bytes 134217728 | tf_op jit(solution)/shard_map/concatenate | solution.py:46
  (14 shorter events, 0.0 us)
Async XLA Ops:
  6.5 80.3 %all-reduce.3.cloned.1.call-start = ((), (), s32[]{:S(2)}) async-start(), calls=%async_computation | async-start | bytes 3211264 | tf_op jit(solution)/shard_map/psum | solution.py:13
  48.4 19.8 %copy-start.4 = (f32[16]{0:T(128)S(1)}, f32[16]{0:T(128)}, u32[]{:S(2)}) copy-start(f32[16]{0:T(128)} %param.3) | copy-start | bytes 196
  181.7 5.9 %copy-start.3 = (bf16[512,353]{0,1:T(8,128)(2,1)S(1)}, bf16[512,353]{0,1:T(8,128)(2,1)}, u32[]{:S(2)}) copy-start(bf16[512,353]{0,1:T(8,128)(2,1)} %fusion.24) | copy-start | bytes 1084420
  182.5 2.6 copy-start
  185.1 2.5 copy-start.2
  192.8 9.1 %copy-start.1 = (bf16[8,1024,353]{1,2,0:T(8,128)(2,1)S(1)}, bf16[8,1024,353]{1,2,0:T(8,128)(2,1)}, u32[]{:S(2)}) copy-start(bf16[8,1024,353]{1,2,0:T(8,128)(2,1)} %copy-done) | copy-start | bytes 17350660
  192.8 17.5 %slice-start = ((s8[5898240]{0:T(1024)(128)(4,1)}), s8[1703936]{0:T(1024)(128)(4,1)S(1)}, s32[]{:S(2)}) async-start(s8[5898240]{0:T(1024)(128)(4,1)} %bitcast.165), calls=%async_computation.1 | async-start | bytes 3407872
  201.9 8.5 %slice-start.1 = ((s8[5898240]{0:T(1024)(128)(4,1)}), s8[4194304]{0:T(1024)(128)(4,1)S(1)}, s32[]{:S(2)}) async-start(s8[5898240]{0:T(1024)(128)(4,1)} %bitcast.165), calls=%async_computation.2 | async-start | bytes 8388608
Sparse Core Ops, SparseCore 0:
  28.8 58.0 all-reduce.2
where the time goes:
time: 334 us; the launch traced here: 332 us
  local copies, waits for them, and re-layouts  183 us (55%)
  other arithmetic  82.7 us (25%)
  matrix products  31.1 us (9%)
  blocking collectives  20.8 us (6%)
  between operations  13.6 us (4%)
    slice x33, local copies, waits for them, and re-layouts, whiten(): decimated = decimated + taps[k] * samples[:, k:k + 2 * count - 1:2]  109 us
    concatenate x1, local copies, waits for them, and re-layouts, on_device(): return jnp.concatenate(groups, axis=0)  65.8 us
    concatenate x1, other arithmetic, on_device(): return jnp.concatenate(groups, axis=0)  40.9 us
    reduce_sum x2, other arithmetic, whiten(): centred = decimated - jnp.mean(decimated, axis=1, keepdims=True)  37.2 us
    dot_general x4, matrix products, on_device(): jnp.einsum('in,ljn->lij', left, shifted, preferred_element_type=jnp.float32)  31.1 us
    all_gather x1, blocking collectives, on_device(): source = lax.all_gather(traces, 'col', axis=0, tiled=True)  20.8 us
    unnamed x21, local copies, waits for them, and re-layouts  7.78 us
  transfers between devices with their start and end apart: 1, of which 1 were waited for; matrix products, arithmetic and copies ran while one was open for 17% of the time, Pallas kernels for 0%

commit v1 on v0

v1 whole, which is shorter than its diff:
```python
import functools
import math

import jax
import jax.numpy as jnp
from jax import lax
from jax.experimental import pallas as pl
from jax.experimental.pallas import tpu as pltpu
from jax.sharding import PartitionSpec as P

LAGS = 32
MESH = pl.DeviceIdType.MESH


def whiten(x_ref, taps_ref, count):
    taps = taps_ref.shape[0]
    tile = 128
    depth = 2 * tile + taps - 2
    m = lax.broadcasted_iota(jnp.int32, (depth, tile), 0)
    n = lax.broadcasted_iota(jnp.int32, (depth, tile), 1)
    offset = m - 2 * n
    band = jnp.zeros((depth, tile), jnp.float32)
    for k in range(taps):
        band = jnp.where(offset == k, taps_ref[k], band)
    high = band.astype(jnp.bfloat16)
    rest = band - high.astype(jnp.float32)
    middle = rest.astype(jnp.bfloat16)
    low = (rest - middle.astype(jnp.float32)).astype(jnp.bfloat16)
    pieces = []
    for t in range(count // tile):
        x = x_ref[:, 2 * tile * t : 2 * tile * t + depth]
        total = jnp.dot(x, low, preferred_element_type=jnp.float32)
        total += jnp.dot(x, middle, preferred_element_type=jnp.float32)
        total += jnp.dot(x, high, preferred_element_type=jnp.float32)
        pieces.append(total)
    decimated = jnp.concatenate(pieces, axis=1)
    centred = decimated - jnp.mean(decimated, axis=1, keepdims=True)
    spread = jnp.sqrt(jnp.mean(centred * centred, axis=1, keepdims=True) + 1e-06)
    return (centred / spread).astype(jnp.bfloat16)


def gather_kernel(R, C, count, x_ref, taps_ref, first, second, send1, recv1, send2, recv2, sendp, recvp):
    r = lax.axis_index("row")
    c = lax.axis_index("col")
    block = r * C + c
    to_r, to_c = lax.rem(block, R), lax.div(block, R)
    wanted = c * R + r
    from_r, from_c = lax.div(wanted, C), lax.rem(wanted, C)
    fixed = wanted == block

    barrier = pltpu.get_barrier_semaphore()

    def greet(row, col):
        pl.semaphore_signal(barrier, inc=1, device_id=(row, col), device_id_type=MESH)

    for k in range(1, R):
        greet(lax.rem(r + k, R), c)
    for k in range(1, C):
        greet(r, lax.rem(c + k, C))

    @pl.when(jnp.logical_not(fixed))
    def _():
        greet(to_r, to_c)
        greet(from_r, from_c)

    mine = whiten(x_ref, taps_ref, count)
    first[pl.ds(c, 1)] = mine[None]

    @pl.when(fixed)
    def _():
        second[pl.ds(r, 1)] = mine[None]

    pl.semaphore_wait(barrier, R - 1 + C - 1 + jnp.where(fixed, 0, 2))

    def swap():
        return pltpu.make_async_remote_copy(
            first.at[c], second.at[to_r], sendp, recvp, device_id=(to_r, to_c), device_id_type=MESH)

    def arrived_swap():
        return pltpu.make_async_remote_copy(
            first.at[c], second.at[r], sendp, recvp, device_id=(to_r, to_c), device_id_type=MESH)

    def col_copy(slot, col, way):
        return pltpu.make_async_remote_copy(
            first.at[slot], first.at[slot], send1.at[way, slot], recv1.at[slot],
            device_id=(r, col), device_id_type=MESH)

    def row_copy(slot, row, k):
        return pltpu.make_async_remote_copy(
            second.at[slot], second.at[slot], send2.at[k], recv2.at[slot],
            device_id=(row, c), device_id_type=MESH)

    @pl.when(jnp.logical_not(fixed))
    def _():
        swap().start()

    @pl.when(c + 1 < C)
    def _():
        col_copy(c, c + 1, 0).start()

    @pl.when(c >= 1)
    def _():
        col_copy(c, c - 1, 1).start()

    @pl.when(jnp.logical_not(fixed))
    def _():
        arrived_swap().wait_recv()

    half = R // 2
    core = lax.rem(r, 2)
    chip = lax.div(r, 2)
    partner = r + 1 - 2 * core
    for k in list(range(1, half)):
        row_copy(r, 2 * lax.rem(chip + k, half) + core, k).start()
    row_copy(r, partner, 0).start()

    for step in range(1, max(half, C)):
        if step < C:
            left, right = c - step, c + step

            @pl.when(left >= 0)
            def _():
                col_copy(left, c, 0).wait_recv()

                @pl.when(c + 1 < C)
                def _():
                    col_copy(left, c + 1, 0).start()

            @pl.when(right < C)
            def _():
                col_copy(right, c, 1).wait_recv()

                @pl.when(c >= 1)
                def _():
                    col_copy(right, c - 1, 1).start()

        if step < half:
            slot = 2 * lax.rem(chip + half - step, half) + core
            row_copy(slot, partner, 0).wait_recv()
            row_copy(slot, partner, half + step).start()

    for k in range(half):
        slot = 2 * lax.rem(chip + k, half) + 1 - core
        row_copy(slot, partner, 0).wait_recv()

    for k in range(half):
        row_copy(r, partner, k).wait_send()
    for k in range(1, half):
        row_copy(r, partner, half + k).wait_send()

    @pl.when(jnp.logical_not(fixed))
    def _():
        swap().wait_send()

    for slot in range(C):
        @pl.when(jnp.logical_and(slot <= c, c + 1 < C))
        def _():
            col_copy(slot, c + 1, 0).wait_send()

        @pl.when(jnp.logical_and(slot >= c, c >= 1))
        def _():
            col_copy(slot, c - 1, 1).wait_send()


def gather(R, C, count, traces, taps):
    rows = traces.shape[0]
    vmem = pl.BlockSpec(memory_space=pltpu.VMEM)
    return pl.pallas_call(
        functools.partial(gather_kernel, R, C, count),
        out_shape=(
            jax.ShapeDtypeStruct((C, rows, count), jnp.bfloat16),
            jax.ShapeDtypeStruct((R, rows, count), jnp.bfloat16),
        ),
        in_specs=[vmem, pl.BlockSpec(memory_space=pltpu.SMEM)],
        out_specs=(vmem, vmem),
        scratch_shapes=[
            pltpu.SemaphoreType.DMA((2, C)),
            pltpu.SemaphoreType.DMA((C,)),
            pltpu.SemaphoreType.DMA((R,)),
            pltpu.SemaphoreType.DMA((R,)),
            pltpu.SemaphoreType.DMA,
            pltpu.SemaphoreType.DMA,
        ],
        compiler_params=pltpu.CompilerParams(
            collective_id=0, has_side_effects=True, vmem_limit_bytes=32 * 1024 * 1024),
        name="whiten_gather",
    )(traces, taps)


def correlate_kernel(width, per_step, first, second, out, left, right, lagged):
    rows = left.shape[0]

    @pl.when(pl.program_id(0) == 0)
    def _():
        n = lax.broadcasted_iota(jnp.int32, left.shape, 1)
        left[...] = jnp.where(n < width, first[...].astype(jnp.float32), 0.0)
        right[...] = second[...].T

    scale = 1.0 / math.sqrt(width)
    x = left[...]
    for k in range(per_step):
        lagged[k * rows : (k + 1) * rows] = x.astype(jnp.bfloat16)
        x = pltpu.roll(x, 1, 1)
    left[...] = x
    product = jnp.dot(lagged[...], right[...], preferred_element_type=jnp.float32) * scale
    out[...] = product.reshape(out.shape)


def correlate(first, second, width, per_step=4):
    rows, count = first.shape
    columns = second.shape[0]
    return pl.pallas_call(
        functools.partial(correlate_kernel, width, per_step),
        out_shape=jax.ShapeDtypeStruct((LAGS, rows, columns), jnp.float32),
        grid=(LAGS // per_step,),
        in_specs=[
            pl.BlockSpec((rows, count), lambda s: (0, 0)),
            pl.BlockSpec((columns, count), lambda s: (0, 0)),
        ],
        out_specs=pl.BlockSpec((per_step, rows, columns), lambda s: (s, 0, 0)),
        scratch_shapes=[
            pltpu.VMEM((rows, count), jnp.float32),
            pltpu.VMEM((count, columns), jnp.bfloat16),
            pltpu.VMEM((per_step * rows, count), jnp.bfloat16),
        ],
        compiler_params=pltpu.CompilerParams(vmem_limit_bytes=48 * 1024 * 1024),
        cost_estimate=pl.CostEstimate(
            flops=2 * LAGS * rows * columns * count,
            bytes_accessed=4 * LAGS * rows * columns, transcendentals=0),
        name="correlate",
    )(first, second)


def solution(mesh):
    R, C = mesh.shape["row"], mesh.shape["col"]

    def on_device(traces, taps):
        count = (traces.shape[1] - taps.shape[0] + 2) // 2
        width = count - LAGS + 1
        first, second = gather(R, C, count, traces, taps)
        first = first.reshape(-1, count)
        second = second.reshape(-1, count)
        return correlate(first, second, width)

    placed = (P(("row", "col"), None), P())
    return jax.shard_map(
        on_device, mesh=mesh, in_specs=placed, out_specs=P(None, "row", "col"), check_vma=False
    )
```

time: 334 us -> 50.6 us (0.15)
  local copies, waits for them, and re-layouts: 183 us -> 1.73 us
  other arithmetic: 82.7 us -> 0 us
  Pallas kernels: 0 us -> 48.7 us
  matrix products: 31.1 us -> 0 us
  blocking collectives: 20.8 us -> 0 us
  between operations: 13.6 us -> 0.02 us
    slice x33 -> x0, local copies, waits for them, and re-layouts: 109 us -> none  [whiten(): decimated = decimated + taps[k] * samples[:, k:k + 2 * count - 1:2]]
    concatenate x1 -> x0, local copies, waits for them, and re-layouts: 65.8 us -> none  [on_device(): return jnp.concatenate(groups, axis=0)]
    pallas_call x0 -> x2, Pallas kernels: none -> 48.7 us  [the longest x1 26.5 us: correlate(): pl.pallas_call(functools.partial(correlate_kernel, width, per_step), out_...]
    concatenate x1 -> x0, other arithmetic: 40.9 us -> none  [on_device(): return jnp.concatenate(groups, axis=0)]
    reduce_sum x4 -> x0, other arithmetic: 37.6 us -> none  [the longest x2 37.2 us: whiten(): centred = decimated - jnp.mean(decimated, axis=1, keepdims=True)]
    dot_general x4 -> x0, matrix products: 31.1 us -> none  [on_device(): jnp.einsum('in,ljn->lij', left, shifted, preferred_element_type=jnp.float32)]
    all_gather x1 -> x0, blocking collectives: 20.8 us -> none  [on_device(): source = lax.all_gather(traces, 'col', axis=0, tiled=True)]
    unnamed x21 -> x3, local copies, waits for them, and re-layouts: 7.78 us -> 1.73 us
  transfers between devices with their start and end apart: 1 -> 0, of which waited for: 1 -> 0; matrix products, arithmetic and copies ran while one was open for 17% -> 0% of each run, Pallas kernels for 0% -> 0%
where the time goes in v1:
time: 50.6 us; the launch traced here: 50.5 us
  Pallas kernels  48.7 us (96%)
  local copies, waits for them, and re-layouts  1.73 us (3%)
    pallas_call x1, Pallas kernels, correlate(): pl.pallas_call(functools.partial(correlate_kernel, width, per_step), out_...  26.5 us
    pallas_call x1, Pallas kernels, gather(): pl.pallas_call(functools.partial(gather_kernel, R, C, count), out_shape=(...  22.2 us
    unnamed x3, local copies, waits for them, and re-layouts  1.73 us

profile of v1, /device:TPU:0, one launch (start us, length us, event | category | flops | bytes accessed | tf_op | source)
XLA Modules:
  0.0 50.5 jit_solution(15241152957500680582)
XLA Ops:
  0.0 1.1 %copy.3.x_ref = bf16[128,782]{1,0:T(8,128)(2,1)S(1)} copy(bf16[128,782]{0,1:T(8,128)(2,1)} %param.2) | data formatting | bytes 400384 | tf_op args[0]
  1.1 0.0 copy-start
  1.1 0.6 %copy-done = f32[16]{0:T(128)S(1)} copy-done((f32[16]{0:T(128)S(1)}, f32[16]{0:T(128)}, u32[]{:S(2)}) %copy-start) | copy-done | bytes 88
  1.7 22.2 %whiten_gather.1 = (bf16[4,128,384]{2,1,0:T(8,128)(2,1)S(1)}, bf16[8,128,384]{2,1,0:T(8,128)(2,1)S(1)}) custom-call(bf16[128,782]{1,0:T(8,128)(2,1)S(1)} %copy.3.x_ref, f32[16]{0:T(128)S(1)} %copy-done), custom_call_target="tpu_custom_call" | custom-call | tf_op jit(solution)/shard_map/whiten_gather/pallas_call | solution.py:168
  24.0 26.5 %correlate.1 = f32[32,512,1024]{2,1,0:T(8,128)} custom-call(bf16[512,384]{1,0:T(8,128)(2,1)S(1)} %bitcast.3, bf16[1024,384]{1,0:T(8,128)(2,1)S(1)} %bitcast.2), custom_call_target="tpu_custom_call" | custom-call | flops 12884901888 | bytes 67108864 | tf_op jit(solution)/shard_map/correlate/pallas_call | solution.py:212
Async XLA Ops:
  1.1 0.7 %copy-start = (f32[16]{0:T(128)S(1)}, f32[16]{0:T(128)}, u32[]{:S(2)}) copy-start(f32[16]{0:T(128)} %taps_ref.1) | copy-start | bytes 196

commit v2 on v1

--- a/solution.py
+++ b/solution.py
@@ -26,12 +26,13 @@
     rest = band - high.astype(jnp.float32)
     middle = rest.astype(jnp.bfloat16)
     low = (rest - middle.astype(jnp.float32)).astype(jnp.bfloat16)
+    over_samples = (((0,), (0,)), ((), ()))
     pieces = []
     for t in range(count // tile):
-        x = x_ref[:, 2 * tile * t : 2 * tile * t + depth]
-        total = jnp.dot(x, low, preferred_element_type=jnp.float32)
-        total += jnp.dot(x, middle, preferred_element_type=jnp.float32)
-        total += jnp.dot(x, high, preferred_element_type=jnp.float32)
+        x = x_ref[2 * tile * t : 2 * tile * t + depth]
+        total = lax.dot_general(x, low, over_samples, preferred_element_type=jnp.float32)
+        total += lax.dot_general(x, middle, over_samples, preferred_element_type=jnp.float32)
+        total += lax.dot_general(x, high, over_samples, preferred_element_type=jnp.float32)
         pieces.append(total)
     decimated = jnp.concatenate(pieces, axis=1)
     centred = decimated - jnp.mean(decimated, axis=1, keepdims=True)
@@ -114,30 +115,29 @@
         row_copy(r, 2 * lax.rem(chip + k, half) + core, k).start()
     row_copy(r, partner, 0).start()
 
-    for step in range(1, max(half, C)):
-        if step < C:
-            left, right = c - step, c + step
-
-            @pl.when(left >= 0)
+    for step in range(1, C):
+        left, right = c - step, c + step
+
+        @pl.when(left >= 0)
+        def _():
+            col_copy(left, c, 0).wait_recv()
+
+            @pl.when(c + 1 < C)
             def _():
-                col_copy(left, c, 0).wait_recv()
-
-                @pl.when(c + 1 < C)
-                def _():
-                    col_copy(left, c + 1, 0).start()
-
-            @pl.when(right < C)
+                col_copy(left, c + 1, 0).start()
+
+        @pl.when(right < C)
+        def _():
+            col_copy(right, c, 1).wait_recv()
+
+            @pl.when(c >= 1)
             def _():
-                col_copy(right, c, 1).wait_recv()
-
-                @pl.when(c >= 1)
-                def _():
-                    col_copy(right, c - 1, 1).start()
-
-        if step < half:
-            slot = 2 * lax.rem(chip + half - step, half) + core
-            row_copy(slot, partner, 0).wait_recv()
-            row_copy(slot, partner, half + step).start()
+                col_copy(right, c - 1, 1).start()
+
+    for step in range(1, half):
+        slot = 2 * lax.rem(chip + half - step, half) + core
+        row_copy(slot, partner, 0).wait_recv()
+        row_copy(slot, partner, half + step).start()
 
     for k in range(half):
         slot = 2 * lax.rem(chip + k, half) + 1 - core
@@ -163,7 +163,7 @@
 
 
 def gather(R, C, count, traces, taps):
-    rows = traces.shape[0]
+    rows = traces.shape[1]
     vmem = pl.BlockSpec(memory_space=pltpu.VMEM)
     return pl.pallas_call(
         functools.partial(gather_kernel, R, C, count),
@@ -237,7 +237,7 @@
     def on_device(traces, taps):
         count = (traces.shape[1] - taps.shape[0] + 2) // 2
         width = count - LAGS + 1
-        first, second = gather(R, C, count, traces, taps)
+        first, second = gather(R, C, count, traces.T, taps)
         first = first.reshape(-1, count)
         second = second.reshape(-1, count)
         return correlate(first, second, width)

time: 50.6 us -> 50.7 us (level)
    unnamed x3 -> x4, local copies, waits for them, and re-layouts: 1.73 us -> 1.58 us
where the time goes in v2:
time: 50.7 us; the launch traced here: 50.6 us
  Pallas kernels  49 us (97%)
  local copies, waits for them, and re-layouts  1.58 us (3%)
    pallas_call x1, Pallas kernels, correlate(): pl.pallas_call(functools.partial(correlate_kernel, width, per_step), out_...  26.5 us
    pallas_call x1, Pallas kernels, gather(): pl.pallas_call(functools.partial(gather_kernel, R, C, count), out_shape=(...  22.5 us
    unnamed x4, local copies, waits for them, and re-layouts  1.58 us

profile of v2, /device:TPU:0, one launch (start us, length us, event | category | flops | bytes accessed | tf_op | source)
XLA Modules:
  0.0 50.6 jit_solution(9934463747272128916)
XLA Ops:
  0.0 0.0 copy-start
  0.0 0.9 %copy-done = bf16[128,782]{0,1:T(8,128)(2,1)S(1)} copy-done((bf16[128,782]{0,1:T(8,128)(2,1)S(1)}, bf16[128,782]{0,1:T(8,128)(2,1)}, u32[]{:S(2)}) %copy-start) | copy-done | bytes 200216
  0.9 0.0 copy-start.1
  0.9 0.7 %copy-done.1 = f32[16]{0:T(128)S(1)} copy-done((f32[16]{0:T(128)S(1)}, f32[16]{0:T(128)}, u32[]{:S(2)}) %copy-start.1) | copy-done | bytes 88
  1.6 22.5 %whiten_gather.1 = (bf16[4,128,384]{2,1,0:T(8,128)(2,1)S(1)}, bf16[8,128,384]{2,1,0:T(8,128)(2,1)S(1)}) custom-call(bf16[782,128]{1,0:T(8,128)(2,1)S(1)} %bitcast.5, f32[16]{0:T(128)S(1)} %copy-done.1), custom_call_target="tpu_custom_call" | custom-call | tf_op jit(solution)/shard_map/whiten_gather/pallas_call | solution.py:168
  24.1 26.5 %correlate.1 = f32[32,512,1024]{2,1,0:T(8,128)} custom-call(bf16[512,384]{1,0:T(8,128)(2,1)S(1)} %bitcast.4, bf16[1024,384]{1,0:T(8,128)(2,1)S(1)} %bitcast.3), custom_call_target="tpu_custom_call" | custom-call | flops 12884901888 | bytes 67108864 | tf_op jit(solution)/shard_map/correlate/pallas_call | solution.py:212
Async XLA Ops:
  0.0 0.9 %copy-start = (bf16[128,782]{0,1:T(8,128)(2,1)S(1)}, bf16[128,782]{0,1:T(8,128)(2,1)}, u32[]{:S(2)}) copy-start(bf16[128,782]{0,1:T(8,128)(2,1)} %param.2) | copy-start | bytes 600580
  0.9 0.7 %copy-start.1 = (f32[16]{0:T(128)S(1)}, f32[16]{0:T(128)}, u32[]{:S(2)}) copy-start(f32[16]{0:T(128)} %taps_ref.1) | copy-start | bytes 196
